TPU v7x, 128 devices: a whole 4x4x4 slice. The times are simulated.
128 devices in a mesh: ctx: 64 (over x, z_hi, y, core), fsdp: 2 (over z_lo).
Axes of the slice: x: 4, y: 4, z: 4 (z_hi: 2, z_lo: 2; z = z_hi * 2 + z_lo), core: 2. Of those that a mesh axis runs over, the one named last changes fastest.
Arguments:
- hidden: bfloat16 [16384, 960], P(('fsdp', 'ctx')), parts along dimension 0, may hold values from -16 to 16
- attn_gain: bfloat16 [1920], P(('fsdp', 'ctx')), parts along dimension 0, may hold values from 0.5 to 1.5
- w_q: bfloat16 [1920, 960], P(('fsdp', 'ctx')), parts along dimension 0, may hold values from -0.1875 to 0.1875
- w_k: bfloat16 [1920, 320], P(('fsdp', 'ctx')), parts along dimension 0, may hold values from -0.1875 to 0.1875
- w_v: bfloat16 [1920, 320], P(('fsdp', 'ctx')), parts along dimension 0, may hold values from -0.1875 to 0.1875
- w_o: bfloat16 [1920, 960], P(('fsdp', 'ctx')), parts along dimension 0, may hold values from -1.5 to 1.5
- mlp_gain: bfloat16 [1920], P(('fsdp', 'ctx')), parts along dimension 0, may hold values from 0.5 to 1.5
- w_gate: bfloat16 [1920, 2560], P(('fsdp', 'ctx')), parts along dimension 0, may hold values from -0.1875 to 0.1875
- w_up: bfloat16 [1920, 2560], P(('fsdp', 'ctx')), parts along dimension 0, may hold values from -0.1875 to 0.1875
- w_down: bfloat16 [5120, 960], P(('fsdp', 'ctx')), parts along dimension 0, may hold values from -0.125 to 0.125
- cotangent: bfloat16 [16384, 960], P(('fsdp', 'ctx')), parts along dimension 0, may hold values from -6 to 6
- doc_lengths: int32 [6], P('fsdp'), parts along dimension 0, may hold values from 1024 to 4096, as said below
- span_order: int32 [128], P('fsdp'), parts along dimension 0, may hold values from 0 to 63, as said below
Outputs:
- output: bfloat16 [16384, 960], P(('fsdp', 'ctx')), parts along dimension 0
- grad_hidden: bfloat16 [16384, 960], P(('fsdp', 'ctx')), parts along dimension 0
- grad_attn_gain: float32 [1920], P(('fsdp', 'ctx')), parts along dimension 0
- grad_w_q: float32 [1920, 960], P(('fsdp', 'ctx')), parts along dimension 0
- grad_w_k: float32 [1920, 320], P(('fsdp', 'ctx')), parts along dimension 0
- grad_w_v: float32 [1920, 320], P(('fsdp', 'ctx')), parts along dimension 0
- grad_w_o: float32 [1920, 960], P(('fsdp', 'ctx')), parts along dimension 0
- grad_mlp_gain: float32 [1920], P(('fsdp', 'ctx')), parts along dimension 0
- grad_w_gate: float32 [1920, 2560], P(('fsdp', 'ctx')), parts along dimension 0
- grad_w_up: float32 [1920, 2560], P(('fsdp', 'ctx')), parts along dimension 0
- grad_w_down: float32 [5120, 960], P(('fsdp', 'ctx')), parts along dimension 0
There are 2 independent parts, one for each index of `fsdp`. A program takes and returns all parts, laid end to end along the dimension named above; each array names one. Nothing has to cross between parts.
Inputs may be any that keep to these rules, and one draw needn't show every extreme that they name: `doc_lengths`: the lengths of the 3 documents in stream order; they sum to 8192 and one of them has 4096 tokens. A permutation of the blocks: rows i * 128 to i * 128 + 127 of every token array are stream positions span_order[i] * 128 onward.
All inputs are finite; a program needn't handle non-finite values.
Results may differ from a plain program's by a relative error of at most 0.033.
Values may be sent and summed in bfloat16 or wider, within the bound.
A program may use at most 256 MiB of HBM per device.

v0:
```python
import jax
import jax.numpy as jnp
import numpy as np
from jax import lax
from jax.experimental import pallas as pl
from jax.experimental.pallas import tpu as pltpu
from jax.sharding import PartitionSpec as P

HEAD = 64
EPSILON = 1e-05
ROPE_BASE = 100000.0
MASKED = -1e30
WIDE = 1024
WIDTH = 960
BF = jnp.bfloat16
F32 = jnp.float32
MESH = pl.DeviceIdType.MESH
DMA = pltpu.SemaphoreType.DMA
ANY = pl.BlockSpec(memory_space=pl.ANY)
VMEM = pl.BlockSpec(memory_space=pltpu.VMEM)
SMEM = pl.BlockSpec(memory_space=pltpu.SMEM)
LIMIT = 56 * 2**20
OWNED_KV = (0, 1, 1, 2, 2, 3, 4, 4)


def dot(a, b):
    return lax.dot_general(a, b, (((1,), (0,)), ((), ())), preferred_element_type=F32)


def dot_nt(a, b):
    return lax.dot_general(a, b, (((1,), (1,)), ((), ())), preferred_element_type=F32)


def dot_tn(a, b):
    return lax.dot_general(a, b, (((0,), (0,)), ((), ())), preferred_element_type=F32)


def shaped(shape, dtype):
    return jax.ShapeDtypeStruct(shape, dtype)


def place():
    i = lax.axis_index("ctx")
    return i // 16, (i // 8) % 2, (i // 2) % 4, i % 2


def at(x, z, y, c):
    return {"ctx": (((x + 4) % 4) * 2 + z) * 8 + ((y + 4) % 4) * 2 + c}


def send(src, dst, ssem, rsem, device):
    copy = pltpu.make_async_remote_copy(
        src, dst, ssem, rsem, device_id=device, device_id_type=MESH
    )
    copy.start()
    return copy


def hail(kinds):
    x, z, y, c = place()
    who = []
    if "x" in kinds:
        who += [at(x + 1, z, y, c), at(x - 1, z, y, c), at(x, 1 - z, y, c)]
    if "f" in kinds:
        who += [at(x, z, y + d, (c + e) % 2) for d in range(4) for e in range(2) if d + e]
    elif "y" in kinds:
        who += [at(x, z, y + d, c) for d in (1, 2, 3)] + [at(x, z, y, 1 - c)]
    barrier = pltpu.get_barrier_semaphore()
    for device in who:
        pl.semaphore_signal(barrier, inc=1, device_id=device, device_id_type=MESH)
    return len(who)


def greet(kinds):
    pl.semaphore_wait(pltpu.get_barrier_semaphore(), hail(kinds))


def half_lead(ref, k):
    n = ref.shape[0] // 2
    return ref.at[pl.ds(k * n, n)]


def half_lanes(ref, k):
    n = ref.shape[-1] // 2
    return ref.at[:, pl.ds(k * n, n)]


class RingGather:
    sems = [DMA((9,)), DMA((9,)), DMA(())]

    def __init__(self, src, dst, half, ssem, rsem, lsem, arrived=None):
        self.src, self.dst, self.half = src, dst, half
        self.ssem, self.rsem, self.lsem = ssem, rsem, lsem
        self.arrived = arrived or (lambda block: None)
        self.copies = {}

    def push(self, n, src, dst, device):
        self.copies[n] = send(src, dst, self.ssem.at[n], self.rsem.at[n], device)

    def start(self):
        x, z, y, c = place()
        me = self.dst.at[x * 2 + z]
        self.push(0, self.src, me, at(x, 1 - z, y, c))
        self.push(1, self.src, me, at(x + 1, z, y, c))
        self.push(2, self.src, me, at(x - 1, z, y, c))
        self.local = pltpu.make_async_copy(self.src, me, self.lsem)
        self.local.start()

    def relay_z(self):
        x, z, y, c = place()
        block = self.dst.at[x * 2 + 1 - z]
        self.copies[0].wait_recv()
        self.push(3, block, block, at(x + 1, z, y, c))
        self.push(4, block, block, at(x - 1, z, y, c))
        self.arrived(x * 2 + 1 - z)

    def relay_x(self, k):
        x, z, y, c = place()
        zz = z if k == 0 else 1 - z
        left, right = ((x + 3) % 4) * 2 + zz, ((x + 1) % 4) * 2 + zz
        self.copies[1 + 2 * k].wait_recv()
        part = self.half(self.dst.at[left], 0)
        self.push(5 + 2 * k, part, part, at(x + 1, z, y, c))
        self.arrived(left)
        self.copies[2 + 2 * k].wait_recv()
        part = self.half(self.dst.at[right], 1)
        self.push(6 + 2 * k, part, part, at(x - 1, z, y, c))
        self.arrived(right)

    def land(self, k):
        x, z, y, c = place()
        zz = z if k == 0 else 1 - z
        self.copies[5 + 2 * k].wait_recv()
        self.copies[6 + 2 * k].wait_recv()
        self.arrived(((x + 2) % 4) * 2 + zz)

    def sent(self):
        for n in range(9):
            self.copies[n].wait_send()

    def finish(self):
        self.local.wait()
        self.sent()


def run_ring_gathers(rings):
    for ring in rings:
        ring.relay_z()
    for k in (0, 1):
        for ring in rings:
            ring.relay_x(k)
    for k in (0, 1):
        for ring in rings:
            ring.land(k)


class RowGather:
    sems = [DMA((8,)), DMA((8,)), DMA(())]

    def __init__(self, src, dst, ssem, rsem, lsem):
        self.src, self.dst = src, dst
        self.ssem, self.rsem, self.lsem = ssem, rsem, lsem
        self.copies = {}

    def push(self, n, src, dst, device):
        self.copies[n] = send(src, dst, self.ssem.at[n], self.rsem.at[n], device)

    def start(self):
        x, z, y, c = place()
        me = self.dst.at[y * 2 + c]
        self.push(1, self.src, me, at(x, z, y + 1, c))
        self.push(2, self.src, me, at(x, z, y - 1, c))
        self.push(0, self.src, me, at(x, z, y, 1 - c))
        self.local = pltpu.make_async_copy(self.src, me, self.lsem)
        self.local.start()

    def relay(self):
        x, z, y, c = place()
        for n, step, side in ((1, 3, 0), (2, 1, 1)):
            self.copies[n].wait_recv()
            block = self.dst.at[((y + step) % 4) * 2 + c]
            part = half_lead(block, side)
            self.push(2 + n, part, part, at(x, z, y + 4 - step, c))
            self.push(4 + n, block, block, at(x, z, y, 1 - c))

    def land(self):
        x, z, y, c = place()
        self.copies[3].wait_recv()
        self.copies[4].wait_recv()
        block = self.dst.at[((y + 2) % 4) * 2 + c]
        self.push(7, block, block, at(x, z, y, 1 - c))

    def finish(self):
        self.local.wait()
        for n in (0, 5, 6, 7):
            self.copies[n].wait_recv()
        for n in range(8):
            self.copies[n].wait_send()


class Swap:
    sems = [DMA((8,)), DMA((8,)), DMA(())]

    def __init__(self, src, dst, ssem, rsem, lsem):
        self.src, self.dst = src, dst
        self.ssem, self.rsem, self.lsem = ssem, rsem, lsem

    def start(self):
        x, z, y, c = place()
        me = y * 2 + c
        self.copies = []
        for d in (2, 1, 3, 0):
            for e in (0, 1):
                if d + e:
                    n = d * 2 + e
                    to = ((y + d) % 4) * 2 + (c + e) % 2
                    self.copies.append(
                        send(
                            self.src.at[to],
                            self.dst.at[me],
                            self.ssem.at[n],
                            self.rsem.at[n],
                            at(x, z, y + d, (c + e) % 2),
                        )
                    )
        self.local = pltpu.make_async_copy(self.src.at[me], self.dst.at[me], self.lsem)
        self.local.start()

    def finish(self):
        self.local.wait()
        for copy in self.copies:
            copy.wait()


class RowSum:
    @staticmethod
    def scratch(shape):
        return [
            pltpu.VMEM((4,) + shape, BF),
            pltpu.VMEM((4,) + shape, BF),
            pltpu.VMEM((4,) + shape, BF),
            DMA((8,)),
            DMA((8,)),
        ]

    def __init__(self, blk, first, mixed, second, ssem, rsem):
        self.blk, self.first, self.mixed, self.second = blk, first, mixed, second
        self.ssem, self.rsem = ssem, rsem
        self.copies = {}

    def push(self, n, src, dst, device):
        self.copies[n] = send(src, dst, self.ssem.at[n], self.rsem.at[n], device)

    def hand(self, d):
        x, z, y, c = place()
        to = ((y + d) % 4) * 2 + 1 - c
        self.push(d, self.blk.at[to], self.first.at[d], at(x, z, y, 1 - c))

    def start(self):
        for d in (2, 1, 3, 0):
            self.hand(d)

    def relay(self):
        x, z, y, c = place()
        for d in (2, 1, 3):
            self.copies[d].wait_recv()
            own = self.blk[((y + d) % 4) * 2 + c].astype(F32)
            self.mixed[d] = (own + self.first[d].astype(F32)).astype(BF)
            self.push(4 + d, self.mixed.at[d], self.second.at[d], at(x, z, y + d, c))

    def total(self):
        x, z, y, c = place()
        self.copies[0].wait_recv()
        total = self.blk[y * 2 + c].astype(F32) + self.first[0].astype(F32)
        for d in (1, 3, 2):
            self.copies[4 + d].wait_recv()
            total = total + self.second[d].astype(F32)
        return total

    def finish(self):
        for n in (0, 1, 2, 3, 5, 6, 7):
            self.copies[n].wait_send()


class RingSum:
    @staticmethod
    def scratch(shape, lanes):
        if lanes:
            part = shape[:-1] + (shape[-1] // 2,)
        else:
            part = (shape[0] // 2,) + shape[1:]
        return [
            pltpu.VMEM((4,) + part, BF),
            pltpu.VMEM((4,) + shape, BF),
            pltpu.VMEM((4,) + shape, BF),
            pltpu.VMEM((2,) + shape, BF),
            DMA((9,)),
            DMA((9,)),
        ]

    def __init__(self, blk, lanes, parts, mixed, heard, across, ssem, rsem):
        self.blk, self.half = blk, half_lanes if lanes else half_lead
        self.parts, self.mixed, self.heard, self.across = parts, mixed, heard, across
        self.ssem, self.rsem = ssem, rsem
        self.copies = {}

    def push(self, n, src, dst, device):
        self.copies[n] = send(src, dst, self.ssem.at[n], self.rsem.at[n], device)

    def start(self, k):
        x, z, y, c = place()
        zz = 1 - z if k == 0 else z
        far = self.blk.at[((x + 2) % 4) * 2 + zz]
        self.push(4 * k, self.half(far, 0), self.parts.at[2 * k], at(x + 1, z, y, c))
        self.push(4 * k + 1, self.half(far, 1), self.parts.at[2 * k + 1], at(x - 1, z, y, c))

    def relay(self, k):
        x, z, y, c = place()
        zz = 1 - z if k == 0 else z
        for side, step in ((0, 1), (1, 3)):
            n = 2 * k + side
            mixed = self.mixed.at[n]
            source = self.blk.at[((x + step) % 4) * 2 + zz]
            mine, other = self.half(source, side), self.half(source, 1 - side)
            self.half(mixed, 1 - side)[...] = other[...]
            self.copies[4 * k + side].wait_recv()
            self.half(mixed, side)[...] = (
                mine[...].astype(F32) + self.parts[n].astype(F32)
            ).astype(BF)
            self.push(4 * k + 2 + side, mixed, self.heard.at[n], at(x + step, z, y, c))

    def total(self, k):
        x, z, y, c = place()
        zz = 1 - z if k == 0 else z
        total = self.blk[x * 2 + zz].astype(F32)
        for side in (0, 1):
            self.copies[4 * k + 2 + side].wait_recv()
            total = total + self.heard[2 * k + side].astype(F32)
        if k == 0:
            self.across[0] = total.astype(BF)
            self.push(8, self.across.at[0], self.across.at[1], at(x, 1 - z, y, c))
            return None
        self.copies[8].wait_recv()
        return total + self.across[1].astype(F32)

    def finish(self):
        for n in range(9):
            self.copies[n].wait_send()


def fetch(src, dst, sem):
    copy = pltpu.make_async_copy(src, dst, sem)
    copy.start()
    return copy


def columns_of_gains(gain1, gain2):
    gap = jnp.zeros((1, 113), F32)
    return jnp.concatenate(
        [
            jnp.concatenate([ref[...].astype(F32).reshape(1, 15), gap], axis=1)
            for ref in (gain1, gain2)
        ]
        + [jnp.zeros((126, 128), F32)],
        axis=0,
    ).T[0:15]


def comm_call(name, number, kernel, out_shape, in_specs, out_specs, scratch, args):
    return pl.pallas_call(
        kernel,
        out_shape=out_shape,
        in_specs=in_specs,
        out_specs=out_specs,
        scratch_shapes=scratch,
        compiler_params=pltpu.CompilerParams(
            collective_id=number, has_side_effects=True, vmem_limit_bytes=LIMIT
        ),
        name=name,
    )(*args)


def split(refs, counts):
    parts, begin = [], 0
    for n in counts:
        parts.append(refs[begin : begin + n])
        begin += n
    return parts


def spread_value(rows):
    j = lax.broadcasted_iota(jnp.int32, (rows, WIDE), 0)
    k = lax.broadcasted_iota(jnp.int32, (rows, WIDE), 1)
    hit = ((k // 16) * 15 + k % 16 == j) & (k % 16 < 15)
    return jnp.where(hit, 1.0, 0.0).astype(BF)


def first(
    hidden_t, cot_t, w_q, w_k, w_v, w_o, w_gate, w_up, w_down, gain1, gain2, lengths, span_order, freq
):
    def kernel(
        hidden_t, cot_t, w_q, w_k, w_v, w_o, w_gate, w_up, w_down, gain1, gain2, lengths, order, freq,
        rows_out, w1_out, wds, wo, cot, w2own, normed_out, q_out, kv2, cos_out, sin_out,
        rows, w1, normed, q_rot, cos_t, sin_t, xp, cp, wp1, wp2, wop, wdp, wos, w1own, kv, outs,
        *sems,
    ):
        a, b, d, e, e2, ac, ao, b2, k0, k1, (hs, hr) = split(sems, (3,) * 10 + (2,))
        x, z, y, c = place()
        partners = hail("xf")

        gains = columns_of_gains(gain1, gain2)
        q = jnp.concatenate([w_q[...].astype(F32), jnp.zeros((15, 64), F32)], axis=1)
        q, k, v = (w * gains[:, 0:1] for w in (q, w_k[...].astype(F32), w_v[...].astype(F32)))
        wp1[...] = jnp.zeros(wp1.shape, BF)
        for f in range(8):
            n = OWNED_KV[f] * 64
            wp1[f, 0:15, 0:128] = q[:, 128 * f : 128 * f + 128].astype(BF)
            wp1[f, 0:15, 128:256] = jnp.concatenate(
                [k[:, n : n + 64], v[:, n : n + 64]], axis=1
            ).astype(BF)
        spread = spread_value(WIDTH)
        xp[...] = dot_tn(hidden_t[...], spread).astype(BF)

        pl.semaphore_wait(pltpu.get_barrier_semaphore(), partners)
        swap = Swap(wp1, w1own, *b)
        swap.start()
        gather = RowGather(xp, rows, *a)
        gather.start()
        wop[...] = jnp.zeros(wop.shape, BF)
        wop[0:15, :] = dot(w_o[...], spread).astype(BF)
        wdp[...] = jnp.zeros(wdp.shape, BF)
        wdp[0:40, :] = dot(w_down[...], spread).astype(BF)
        ring_o = RingGather(wop, wos, half_lanes, *e)
        ring_d = RingGather(wdp, wds, half_lanes, *e2)
        swap.finish()
        ring_1 = RingGather(w1own, w1, half_lead, *d)
        ring_1.start()
        ring_o.start()
        ring_d.start()
        cp[...] = dot_tn(cot_t[...], spread).astype(BF)
        gather.relay()
        gather_c = RowGather(cp, cot, *ac)
        gather_c.start()
        rings = [ring_1, ring_o, ring_d]
        for ring in rings:
            ring.relay_z()

        wp2[...] = jnp.zeros(wp2.shape, BF)
        gap = jnp.zeros((15, 8), F32)
        for m, ref in ((0, w_gate), (384, w_up)):
            w = ref[...].astype(F32) * gains[:, 1:2]
            for f in range(8):
                parts = []
                for g in range(8):
                    n = (8 * g + f) * 40
                    parts += [w[:, n : n + 40], gap]
                wp2[f, 0:15, m : m + 384] = jnp.concatenate(parts, axis=1).astype(BF)
        swap2 = Swap(wp2, w2own, *b2)
        swap2.start()

        for k in (0, 1):
            for ring in rings:
                ring.relay_x(k)

        lane = lanes_of((1, 128))
        sign = jnp.where(lane % 64 < 32, -1.0, 1.0)
        ends = doc_ends(lengths)

        @pl.loop(0, 8)
        def _(n):
            pos = order[(x * 2 + z) * 8 + n] * 128
            pos = pos + lax.broadcasted_iota(jnp.int32, (128, 1), 0)
            angle = (pos - doc_start(pos, ends)).astype(F32) * freq[...]
            part = pl.ds(pl.multiple_of(n * 128, 128), 128)
            cos_t[part, :] = jnp.cos(angle)
            sin_t[part, :] = sign * jnp.sin(angle)

        written = [fetch(cos_t, cos_out, outs.at[0]), fetch(sin_t, sin_out, outs.at[1])]
        gather.land()
        for k in (0, 1):
            for ring in rings:
                ring.land(k)
        ring_o.local.wait()
        gather_o = RowGather(wos, wo, *ao)
        gather_o.start()
        gather.finish()
        ring_1.local.wait()
        written += [fetch(rows, rows_out, outs.at[2]), fetch(w1, w1_out, outs.at[3])]

        w = w1.reshape(WIDE, 256)
        lane = lanes_of((256, 128))

        def project(n):
            part = pl.ds(n * 256, 256)
            xs = jnp.concatenate([rows[2 * n], rows[2 * n + 1]], axis=0).astype(F32)
            v = (xs * inverse_rms(xs)).astype(BF)
            normed[part, :] = v
            out = dot(v, w[...])
            cos_v, sin_v = cos_t[part, :], sin_t[part, :]
            qs, ks = out[:, 0:128], out[:, 128:256]
            qs = (qs * cos_v + partner(qs) * sin_v).astype(BF).astype(F32) * 0.125
            kv[part, :] = jnp.where(lane < 64, ks * cos_v + partner(ks) * sin_v, ks).astype(BF)
            q_rot[0, part, :] = jnp.where(lane < 64, qs, 0.0).astype(BF)
            q_rot[1, part, :] = jnp.where(lane < 64, pltpu.roll(qs, 64, 1), 0.0).astype(BF)

        hand = []

        def pass_on(piece):
            n = len(hand)
            hand.append(send(piece, piece, hs.at[n], hr.at[n], at(x, z, y, 1 - c)))

        key_rings = []
        for h, own in ((0, k0), (1, k1)):
            mine = kv.at[pl.ds(512 * h, 512)]
            spot = pl.ds(512 * h, 512)
            ring = RingGather(
                mine,
                kv2.at[c, :, spot],
                half_lead,
                *own,
                arrived=lambda block, spot=spot: pass_on(kv2.at[c, block, spot]),
            )
            project(2 * h)
            project(2 * h + 1)
            ring.start()
            n = len(hand)
            hand.append(
                send(
                    mine, kv2.at[c, x * 2 + z, spot], hs.at[n], hr.at[n], at(x, z, y, 1 - c)
                )
            )
            key_rings.append(ring)
            if h == 0:
                gather_c.relay()

        written += [fetch(normed, normed_out, outs.at[4]), fetch(q_rot, q_out, outs.at[5])]
        for ring in key_rings:
            ring.relay_z()
        gather_o.relay()
        for ring in key_rings:
            ring.relay_x(0)
        gather_c.land()
        for ring in key_rings:
            ring.relay_x(1)
        gather_o.land()
        for k in (0, 1):
            for ring in key_rings:
                ring.land(k)
        for copy in hand:
            copy.wait()
        swap2.finish()
        gather_o.finish()
        gather_c.finish()
        for ring in [ring_d] + key_rings:
            ring.finish()
        for ring in (ring_1, ring_o):
            ring.sent()
        for copy in written:
            copy.wait()

    return comm_call(
        "first",
        1,
        kernel,
        (
            shaped((8, 128, WIDE), BF),
            shaped((8, 8, 16, 256), BF),
            shaped((8, 48, WIDE), BF),
            shaped((8, 8, 16, WIDE), BF),
            shaped((8, 128, WIDE), BF),
            shaped((8, 16, 768), BF),
            shaped((1024, WIDE), BF),
            shaped((2, 1024, 128), BF),
            shaped((2, 8, 1024, 128), BF),
            shaped((1024, 128), F32),
            shaped((1024, 128), F32),
        ),
        [VMEM] * 11 + [SMEM, SMEM, VMEM],
        (ANY,) * 11,
        [
            pltpu.VMEM((8, 128, WIDE), BF),
            pltpu.VMEM((8, 8, 16, 256), BF),
            pltpu.VMEM((1024, WIDE), BF),
            pltpu.VMEM((2, 1024, 128), BF),
            pltpu.VMEM((1024, 128), F32),
            pltpu.VMEM((1024, 128), F32),
            pltpu.VMEM((128, WIDE), BF),
            pltpu.VMEM((128, WIDE), BF),
            pltpu.VMEM((8, 16, 256), BF),
            pltpu.VMEM((8, 16, 768), BF),
            pltpu.VMEM((16, WIDE), BF),
            pltpu.VMEM((48, WIDE), BF),
            pltpu.VMEM((8, 16, WIDE), BF),
            pltpu.VMEM((8, 16, 256), BF),
            pltpu.VMEM((1024, 128), BF),
            DMA((6,)),
        ]
        + RowGather.sems
        + Swap.sems
        + RingGather.sems * 3
        + RowGather.sems * 2
        + Swap.sems
        + RingGather.sems * 2
        + [DMA((16,)), DMA((16,))],
        (
            hidden_t, cot_t, w_q, w_k, w_v, w_o, w_gate, w_up, w_down, gain1, gain2, lengths,
            span_order, freq,
        ),
    )


def inverse_rms(v):
    return lax.rsqrt(jnp.sum(v * v, axis=1, keepdims=True) * (1.0 / WIDTH) + EPSILON)


def feed(att, w2own, wo, rows, wd, cot):
    def kernel(
        att, w2own, wo_in, rows_in, wd_in, cot_in,
        output, d_resid, d_heads, gwo_out, gw2_sum, gwd_sum,
        wo, x_in, wd, cot, ins, atts, w2, packed, d_act, resid, normed, act, d_both, dmn, outp,
        gw2, gwd, da, gwo, *refs,
    ):
        a, b, s, r1, r2, t1, t2 = split(refs, (3, 3, 3, 5, 5, 6, 6))
        x, z, y, c = place()
        me = y * 2 + c
        partners = hail("xf")
        pairs = ((wo_in, wo), (cot_in, cot), (wd_in, wd), (rows_in, x_in))
        held = [fetch(src, dst, ins.at[n]) for n, (src, dst) in enumerate(pairs)]
        pl.semaphore_wait(pltpu.get_barrier_semaphore(), partners)
        gather = RowGather(att, atts, *a)
        ring = RingGather(w2own, w2, half_lead, *b)
        gather.start()
        ring.start()

        def place_rows(n, size):
            return pl.ds(pl.multiple_of(n * size, size), size)

        held[0].wait()
        whole = jnp.concatenate([wo[f, g] for g in range(8) for f in range(8)], axis=0)

        def pack(n):
            j = lax.broadcasted_iota(jnp.int32, (512, WIDE), 0) + n * 512
            k = lax.broadcasted_iota(jnp.int32, (512, WIDE), 1)
            hit = ((k // 16) * 15 + k % 16 == j) & (k % 16 < 15)
            packed[pl.ds(n * 512, 512), :] = dot(
                jnp.where(hit, 1.0, 0.0).astype(BF), whole
            ).astype(BF)

        pack(0)
        ring.relay_z()
        gather.relay()
        pack(1)
        ring.relay_x(0)
        held[1].wait()
        held[2].wait()

        @pl.loop(0, 2)
        def _(n):
            part = place_rows(n, 512)
            d_act[part, :] = dot_nt(cot[part, :], wd[...])

        ring.relay_x(1)
        held[3].wait()
        gather.land()
        gather.finish()

        @pl.loop(0, 2)
        def _(n):
            part = place_rows(n, 512)
            heads = jnp.concatenate([atts[f, part, :] for f in range(8)], axis=1)
            v = x_in[part, :].astype(F32) + dot(heads, packed[...])
            resid[part, :] = v
            normed[part, :] = (v * inverse_rms(v)).astype(BF)

        ring.land(0)
        ring.land(1)
        ring.finish()
        w2_all = w2.reshape(WIDE, 768)

        @pl.loop(0, 2)
        def _(n):
            part = place_rows(n, 512)
            both = dot(normed[part, :], w2_all[...])
            gate, up = both[:, 0:384], both[:, 384:768]
            sigma = 1.0 / (1.0 + jnp.exp(-gate))
            silu = gate * sigma
            act[part, :] = (silu * up).astype(BF)
            d = d_act[part, :]
            d_both[part, 0:384] = (d * up * sigma * (1.0 + gate * (1.0 - sigma))).astype(BF)
            d_both[part, 384:768] = (d * silu).astype(BF)

        sum_n, sum_o = RowSum(dmn, *r1), RowSum(outp, *r2)
        ring_2, ring_d = RingSum(gw2, False, *t1), RingSum(gwd, True, *t2)

        def back(core):
            to = [((y + n) % 4) * 2 + core for n in (2, 1, 3, 0)]
            v = jnp.concatenate([d_both[place_rows(n, 128), :] for n in to], axis=0)
            v = dot_nt(v, w2_all[...]).astype(BF)
            for n in range(4):
                dmn[to[n]] = v[128 * n : 128 * n + 128]

        order = [(2, 1), (2, 0), (1, 1), (3, 1), (1, 0), (3, 0), (0, 1), (0, 0)]
        where = [((x + p) % 4) * 2 + (1 - z if q else z) for p, q in order]

        def weights(which):
            v = jnp.concatenate([normed[:, place_rows(where[n], 128)] for n in which], axis=1)
            v = dot_tn(v, d_both[...]).astype(BF)
            for n, m in enumerate(which):
                gw2[where[m]] = v[128 * n : 128 * n + 128].reshape(8, 16, 768)

        weights((0, 1))
        ring_2.start(0)
        ring_2.start(1)
        back(1 - c)
        for d in (2, 1, 3, 0):
            sum_n.hand(d)
        gwd[...] = dot_tn(act[...], cot[...]).astype(BF).reshape(8, 48, WIDE)
        ring_d.start(0)
        ring_d.start(1)
        back(c)
        sum_n.relay()
        weights((2, 3, 4, 5, 6, 7))
        ring_2.relay(0)
        ring_d.relay(0)

        @pl.loop(0, 2)
        def _(n):
            v = dot(act[place_rows(n, 512), :], wd[...]).astype(BF)
            for k in range(4):
                outp[n * 4 + k] = v[128 * k : 128 * k + 128]

        sum_o.start()
        ring_2.relay(1)
        ring_d.relay(1)
        sum_o.relay()

        mine = place_rows(me, 128)
        v = resid[mine, :]
        inv = inverse_rms(v)
        e = sum_n.total()
        mean = jnp.sum(e * v, axis=1, keepdims=True) * (1.0 / WIDTH)
        d_v = cot[mine, :].astype(F32) + inv * e - v * (inv * inv * inv * mean)
        d_resid[...] = d_v
        mixed = d_v.astype(BF)
        d_att = dot_nt(mixed, packed[...]).astype(BF)
        for f in range(8):
            da[f] = d_att[:, f * 128 : (f + 1) * 128]
        swap = Swap(da, d_heads, *s)
        swap.start()
        spread = spread_value(WIDE)
        heads = jnp.concatenate([atts[f, mine, :] for f in range(8)], axis=1)
        gw = dot_tn(dot(heads, spread).astype(BF), mixed).astype(BF)
        for g in range(8):
            for f in range(8):
                n = (8 * g + f) * 16
                gwo[f, g * 16 : (g + 1) * 16, :] = gw[n : n + 16]
        written = fetch(gwo, gwo_out, ins.at[4])
        ring_2.total(0)
        ring_d.total(0)
        output[...] = dot_nt(spread[0:WIDTH], (v + sum_o.total()).astype(BF)).astype(BF)
        gw2_sum[...] = ring_2.total(1).astype(BF)
        gwd_sum[...] = ring_d.total(1)
        swap.finish()
        sum_n.finish()
        sum_o.finish()
        ring_2.finish()
        ring_d.finish()
        written.wait()

    return comm_call(
        "feed",
        3,
        kernel,
        (
            shaped((WIDTH, 128), BF),
            shaped((128, WIDE), F32),
            shaped((8, 128, 128), BF),
            shaped((8, 128, WIDE), BF),
            shaped((8, 16, 768), BF),
            shaped((48, WIDE), F32),
        ),
        [ANY] * 6,
        (VMEM, VMEM, ANY, ANY, VMEM, VMEM),
        [
            pltpu.VMEM((8, 8, 16, WIDE), BF),
            pltpu.VMEM((1024, WIDE), BF),
            pltpu.VMEM((384, WIDE), BF),
            pltpu.VMEM((1024, WIDE), BF),
            DMA((5,)),
            pltpu.VMEM((8, 1024, 128), BF),
            pltpu.VMEM((8, 8, 16, 768), BF),
            pltpu.VMEM((WIDE, WIDE), BF),
            pltpu.VMEM((1024, 384), F32),
            pltpu.VMEM((1024, WIDE), F32),
            pltpu.VMEM((1024, WIDE), BF),
            pltpu.VMEM((1024, 384), BF),
            pltpu.VMEM((1024, 768), BF),
            pltpu.VMEM((8, 128, WIDE), BF),
            pltpu.VMEM((8, 128, WIDE), BF),
            pltpu.VMEM((8, 8, 16, 768), BF),
            pltpu.VMEM((8, 48, WIDE), BF),
            pltpu.VMEM((8, 128, 128), BF),
            pltpu.VMEM((8, 128, WIDE), BF),
        ]
        + RowGather.sems
        + RingGather.sems
        + Swap.sems
        + RowSum.scratch((128, WIDE)) * 2
        + RingSum.scratch((8, 16, 768), False)
        + RingSum.scratch((48, WIDE), True),
        (att, w2own, wo, rows, wd, cot),
    )


def last(
    dkv, gwo, dq, cos_t, sin_t, w1, normed, rows, d_resid, gw2s, gwd, gain1, gain2, w_q, w_k, w_v,
    w_gate, w_up,
):
    def kernel(
        dkv, gwo_in, dq_in, cos_in, sin_in, w1_in, normed_in, rows_in, dr, gw2s, wd, gain1, gain2,
        w_q, w_k, w_v, w_gate, w_up,
        gh, g_attn, g_mlp, g_q, g_k, g_v, g_o, g_gate, g_up, g_down,
        own, gwo, dq, cos_t, sin_t, w1, normed, rows, ins,
        blk, from_core, gwos, gw1, dnq, d_kv, dn, one, two, gw1s, hs, hr, *refs,
    ):
        a, b, d, e, e2, s1, s2 = split(refs, (6, 5, 5, 6, 6, 3, 3))
        x, z, y, c = place()
        me = y * 2 + c
        partners = hail("xf")
        pairs = [
            (gwo_in, gwo),
            (dkv.at[c], own),
            (dq_in, dq),
            (cos_in, cos_t),
            (sin_in, sin_t),
            (w1_in, w1),
            (normed_in, normed),
            (rows_in.at[me], rows),
        ]
        held = [fetch(src, dst, ins.at[n]) for n, (src, dst) in enumerate(pairs)]
        pl.semaphore_wait(pltpu.get_barrier_semaphore(), partners)
        order = [(2, 1), (2, 0), (1, 1), (3, 1), (1, 0), (3, 0), (0, 1), (0, 0)]
        where = [((x + p) % 4) * 2 + (1 - z if q else z) for p, q in order]
        hand = [
            send(dkv.at[1 - c, g], from_core.at[n], hs.at[n], hr.at[n], at(x, z, y, 1 - c))
            for n, g in enumerate(where)
        ]
        held[0].wait()
        sum_w = RowSum(gwo, *b)
        sum_w.start()
        swap2 = Swap(gw2s, two, *s2)
        swap2.start()
        ring = RingSum(blk, False, *a)
        held[1].wait()

        def fold(n):
            g = where[n]
            hand[n].wait_recv()
            blk[g] = (own[g].astype(F32) + from_core[n].astype(F32)).astype(BF)

        fold(0)
        ring.start(0)
        fold(1)
        ring.start(1)
        for n in range(2, 6):
            fold(n)
        sum_w.relay()
        for n in range(2, 6):
            held[n].wait()
        spread = spread_value(WIDTH)
        gains = columns_of_gains(gain1, gain2)

        def place_rows(n, size):
            return pl.ds(pl.multiple_of(n * size, size), size)

        def queries(n):
            part = place_rows(n, 512)
            v = dq[part, :]
            v = (v * cos_t[part, :] - partner(v) * sin_t[part, :]).astype(BF)
            d_kv[part, 0:128] = v
            dnq[part, :] = dot_nt(v, w1[:, 0:128])

        queries(0)
        ring.relay(0)
        queries(1)
        ring.relay(1)
        fold(6)
        fold(7)
        held[6].wait()
        gw1[:, :, :, 0:128] = (
            dot_tn(normed[...], d_kv[:, 0:128]).astype(BF).reshape(8, 8, 16, 128)
        )
        gwos[...] = sum_w.total().astype(BF).reshape(8, 16, WIDE)
        ring_o = RingSum(gwos, True, *e2)
        ring_o.start(0)
        ring_o.start(1)
        ring.total(0)
        swap2.finish()
        total = jnp.zeros((15, 1), F32)
        for m, ref, w in ((0, g_gate, w_gate), (384, g_up, w_up)):
            for n in range(0, 8, 2):
                part = jnp.concatenate(
                    [
                        two[f, :, m + 48 * k : m + 48 * k + 40].astype(F32)[0:15]
                        for k in (n, n + 1)
                        for f in range(8)
                    ],
                    axis=1,
                )
                spot = pl.ds(n * 320, 640)
                ref[:, spot] = part * gains[:, 1:2]
                total += jnp.sum(part * w[:, spot].astype(F32), axis=1, keepdims=True)
        g_mlp[...] = jnp.broadcast_to(total, (15, 128))

        def squeeze(v):
            top = v.astype(BF)
            low = (v - top.astype(F32)).astype(BF)
            return dot_nt(top, spread) + dot_nt(low, spread)

        g_down[...] = squeeze(wd[...])[0:40]
        ring_o.relay(0)
        ring_o.relay(1)

        v = ring.total(1)
        turned = v * cos_t[...] - partner(v) * sin_t[...]
        d_kv[:, 128:256] = jnp.where(lanes_of((1024, 128)) < 64, turned, v).astype(BF)
        sum_n = RowSum(dn, *d)

        def back(core):
            to = [((y + n) % 4) * 2 + core for n in (2, 1, 3, 0)]
            parts = [place_rows(n, 128) for n in to]
            v = jnp.concatenate([d_kv[p, 128:256] for p in parts], axis=0)
            v = dot_nt(v, w1[:, 128:256])
            for n, p in enumerate(parts):
                dn[to[n]] = (dnq[p, :] + v[128 * n : 128 * n + 128]).astype(BF)

        back(1 - c)
        for n in (2, 1, 3, 0):
            sum_n.hand(n)
        ring_1 = RingSum(gw1, False, *e)

        def weights_k(which):
            parts = [place_rows(where[n], 128) for n in which]
            v = jnp.concatenate([normed[:, p] for p in parts], axis=1)
            v = dot_tn(v, d_kv[:, 128:256]).astype(BF)
            for n, m in enumerate(which):
                gw1[where[m], :, :, 128:256] = v[128 * n : 128 * n + 128].reshape(8, 16, 128)

        weights_k((0, 1))
        ring_1.start(0)
        ring_1.start(1)
        back(c)
        sum_n.relay()
        weights_k((2, 3, 4, 5, 6, 7))
        ring_1.relay(0)
        ring_1.relay(1)
        ring_o.total(0)
        ring_1.total(0)
        g_o[...] = squeeze(ring_o.total(1))[0:15]
        gw1s[...] = ring_1.total(1).astype(BF)
        swap1 = Swap(gw1s, one, *s1)
        swap1.start()

        held[7].wait()
        xs = rows[...].astype(F32)
        inv = inverse_rms(xs)
        t = sum_n.total()
        mean = jnp.sum(t * xs, axis=1, keepdims=True) * (1.0 / WIDTH)
        d_x = dr[...] + inv * t - xs * (inv * inv * inv * mean)
        gh[...] = dot_nt(spread, d_x.astype(BF)).astype(BF)
        swap1.finish()
        ones = [one[f].astype(F32)[0:15] for f in range(8)]
        r_q = jnp.concatenate([v[:, 0:128] for v in ones], axis=1)[:, 0:WIDTH]

        def heads(n):
            return jnp.concatenate(
                [
                    sum(ones[f][:, n : n + 64] for f in range(8) if OWNED_KV[f] == h)
                    for h in range(5)
                ],
                axis=1,
            )

        total = jnp.zeros((15, 1), F32)
        for part, w, ref in ((r_q, w_q, g_q), (heads(128), w_k, g_k), (heads(192), w_v, g_v)):
            ref[...] = part * gains[:, 0:1]
            total += jnp.sum(part * w[...].astype(F32), axis=1, keepdims=True)
        g_attn[...] = jnp.broadcast_to(total, (15, 128))
        for copy in hand:
            copy.wait_send()
        ring.finish()
        ring_1.finish()
        ring_o.finish()
        sum_w.finish()
        sum_n.finish()

    return comm_call(
        "last",
        6,
        kernel,
        (
            shaped((WIDTH, 128), BF),
            shaped((15, 128), F32),
            shaped((15, 128), F32),
            shaped((15, WIDTH), F32),
            shaped((15, 320), F32),
            shaped((15, 320), F32),
            shaped((15, WIDTH), F32),
            shaped((15, 2560), F32),
            shaped((15, 2560), F32),
            shaped((40, WIDTH), F32),
        ),
        [ANY] * 8 + [VMEM] * 10,
        (VMEM,) * 10,
        [
            pltpu.VMEM((8, 1024, 128), BF),
            pltpu.VMEM((8, 128, WIDE), BF),
            pltpu.VMEM((1024, 128), F32),
            pltpu.VMEM((1024, 128), F32),
            pltpu.VMEM((1024, 128), F32),
            pltpu.VMEM((WIDE, 256), BF),
            pltpu.VMEM((1024, WIDE), BF),
            pltpu.VMEM((128, WIDE), BF),
            DMA((8,)),
            pltpu.VMEM((8, 1024, 128), BF),
            pltpu.VMEM((8, 1024, 128), BF),
            pltpu.VMEM((8, 16, WIDE), BF),
            pltpu.VMEM((8, 8, 16, 256), BF),
            pltpu.VMEM((1024, WIDE), F32),
            pltpu.VMEM((1024, 256), BF),
            pltpu.VMEM((8, 128, WIDE), BF),
            pltpu.VMEM((8, 16, 256), BF),
            pltpu.VMEM((8, 16, 768), BF),
            pltpu.VMEM((8, 16, 256), BF),
            DMA((8,)),
            DMA((8,)),
        ]
        + RingSum.scratch((1024, 128), False)
        + RowSum.scratch((128, WIDE)) * 2
        + RingSum.scratch((8, 16, 256), False)
        + RingSum.scratch((16, WIDE), True)
        + Swap.sems * 2,
        (
            dkv, gwo, dq, cos_t, sin_t, w1, normed, rows, d_resid, gw2s, gwd, gain1, gain2, w_q,
            w_k, w_v, w_gate, w_up,
        ),
    )


def lanes_of(shape):
    return lax.broadcasted_iota(jnp.int32, shape, len(shape) - 1)


def partner(v):
    lane = lanes_of(v.shape)
    return jnp.where(lane % 64 < 32, pltpu.roll(v, 96, 1), pltpu.roll(v, 32, 1))


def doc_ends(lengths):
    return lengths[0], lengths[0] + lengths[1]


def doc_start(pos, ends):
    return jnp.where(pos < ends[0], 0, jnp.where(pos < ends[1], ends[0], ends[1]))

def layout(order, inverse):
    @pl.loop(0, 64)
    def _(n):
        inverse[order[n]] = n

    i = lax.axis_index("ctx")
    f = i % 8
    upper = (f == 3) | (f == 5)
    return i // 8, (
        jnp.where(upper, 1, 0),
        jnp.where(upper | (f == 1) | (f == 4), 1, 0),
    )


def key_range(span, ends):
    begin = doc_start(span * 128, ends) // 128
    count = span - begin + 1
    runs = (count + 3) // 8
    return begin, runs, jnp.where(count > runs * 8, 1, 0)


def attend(lengths, order, q, kv):
    def kernel(lengths, order, q_ref, kv_ref, o_ref, lse_ref, s_ref, inverse):
        group, sel = layout(order, inverse)
        ends = doc_ends(lengths)

        @pl.loop(0, 8)
        def _(b):
            span = order[group * 8 + b]
            begin, runs, rest = key_range(span, ends)
            pos = span * 128 + lanes_of((1, 256)) % 128
            low = doc_start(pos, ends)
            rows = pl.ds(pl.multiple_of(b * 128, 128), 128)
            none = jnp.zeros((128, 128), BF)
            pair = jnp.concatenate(
                [
                    jnp.concatenate([q_ref[0, rows, :], none], axis=1),
                    jnp.concatenate([none, q_ref[1, rows, :]], axis=1),
                ],
                axis=0,
            )

            def load(h, t, n):
                return jnp.concatenate(
                    [
                        kv_ref[sel[h], pl.ds(inverse[jnp.minimum(t + i, 63)] * 128, 128), :]
                        for i in range(n)
                    ],
                    axis=0,
                )

            def held(t, n):
                return pl.ds(pl.multiple_of((t - begin) * 128, 512), n * 128)

            def scores(n, t, high):
                kpos = t * 128 + lax.broadcasted_iota(jnp.int32, (n * 128, 1), 0)
                allowed = (kpos >= low) & (kpos <= pos)
                keys = jnp.concatenate([load(0, t, n), load(1, t, n)], axis=1)
                s = jnp.where(allowed, dot_nt(keys, pair), MASKED)
                s_ref[held(t, n), :] = s
                return jnp.maximum(high, jnp.max(s.reshape(n * 16, 8, 256), axis=0))

            def over(step, state):
                state = lax.fori_loop(0, runs, lambda j, v: step(8, begin + j * 8, v), state)
                return lax.fori_loop(0, rest, lambda j, v: step(4, begin + runs * 8, v), state)

            high = over(scores, jnp.full((8, 256), MASKED, F32))
            high = jnp.max(high, axis=0, keepdims=True)

            def weigh(n, t, state):
                total, acc = state
                p = jnp.exp(s_ref[held(t, n), :] - high)
                total = total + jnp.sum(p.reshape(n * 16, 8, 256), axis=0)
                values = jnp.where(lanes_of((n * 128, 128)) < 64, pltpu.roll(load(0, t, n), 64, 1), load(1, t, n))
                return total, acc + dot_tn(values, p.astype(BF))

            total, acc = over(weigh, (jnp.zeros((8, 256), F32), jnp.zeros((128, 256), F32)))
            total = jnp.sum(total, axis=0, keepdims=True)
            lse = high + jnp.log(total)
            lse_ref[b, 0:1, :] = lse[:, 0:128]
            lse_ref[b, 1:2, :] = lse[:, 128:256]
            acc = acc / total
            acc = jnp.concatenate([acc[0:64, 0:128], acc[64:128, 128:256]], axis=0)
            o_ref[rows, :] = acc.T.astype(BF)

    return pl.pallas_call(
        kernel,
        in_specs=[SMEM, SMEM, VMEM, VMEM],
        out_specs=(VMEM, VMEM),
        scratch_shapes=[pltpu.VMEM((40 * 128, 256), F32), pltpu.SMEM((64,), jnp.int32)],
        out_shape=(shaped((1024, 128), BF), shaped((8, 8, 128), F32)),
        compiler_params=pltpu.CompilerParams(vmem_limit_bytes=LIMIT),
        name="attend",
    )(lengths, order, q, kv)


def attend_back(lengths, order, q, kv, d_att, att, lse):
    def kernel(
        lengths, order, q_ref, kv_ref, d_ref, o_ref, lse_ref, dq_ref, dkv_ref, acc_ref, inverse
    ):
        lane = lanes_of((128, 128))
        group, sel = layout(order, inverse)
        ends = doc_ends(lengths)

        @pl.loop(0, 16)
        def _(n):
            for s in (0, 1):
                part = pl.ds(pl.multiple_of(n * 512, 512), 512)
                acc_ref[s, part, :] = jnp.zeros((512, 128), F32)

        @pl.loop(0, 8)
        def _(b):
            span = order[group * 8 + b]
            begin, runs, rest = key_range(span, ends)
            pos = span * 128 + lanes_of((1, 128))
            low = doc_start(pos, ends)
            rows = pl.ds(pl.multiple_of(b * 128, 128), 128)
            d_both = d_ref[rows, :].astype(F32)
            d_pad = (
                jnp.where(lane >= 64, pltpu.roll(d_both, 64, 1), 0.0).astype(BF),
                jnp.where(lane >= 64, d_both, 0.0).astype(BF),
            )
            pair = [jnp.concatenate([q_ref[h, rows, :], d_pad[h]], axis=0) for h in (0, 1)]
            mixed = (d_both * o_ref[rows, :].astype(F32)).T
            delta = [jnp.sum(mixed[64 * h : 64 * h + 64], axis=0, keepdims=True) for h in (0, 1)]
            lses = [lse_ref[b, h : h + 1, :] for h in (0, 1)]

            def step(n, t, state):
                where = [inverse[jnp.minimum(t + i, 63)] * 128 for i in range(n)]
                where = [pl.ds(pl.multiple_of(v, 128), 128) for v in where]
                kpos = t * 128 + lax.broadcasted_iota(jnp.int32, (n * 128, 1), 0)
                allowed = (kpos >= low) & (kpos <= pos)
                d_ss, kvs = [], []
                for h in (0, 1):
                    kv_t = jnp.concatenate([kv_ref[sel[h], w, :] for w in where], axis=0)
                    kvs.append(kv_t)
                    both = dot_nt(kv_t, pair[h])
                    p = jnp.where(allowed, jnp.exp(both[:, 0:128] - lses[h]), 0.0)
                    d_s = (p * (both[:, 128:256] - delta[h])).astype(BF)
                    d_ss.append(d_s)
                    d_kv = dot(jnp.concatenate([d_s, p.astype(BF)], axis=1), pair[h])
                    for i, w in enumerate(where):
                        acc_ref[sel[h], w, :] += d_kv[i * 128 : (i + 1) * 128]
                lanes = lanes_of((n * 128, 128))
                keys = jnp.where(lanes < 64, kvs[0], pltpu.roll(kvs[1], 64, 1))
                return state + dot_tn(keys, jnp.concatenate(d_ss, axis=1))

            state = jnp.zeros((128, 256), F32)
            state = lax.fori_loop(0, runs, lambda j, v: step(8, begin + j * 8, v), state)
            state = lax.fori_loop(0, rest, lambda j, v: step(4, begin + runs * 8, v), state)
            state = jnp.concatenate([state[0:64, 0:128], state[64:128, 128:256]], axis=0)
            dq_ref[rows, :] = state.T * 0.125

        @pl.loop(0, 16)
        def _(n):
            for s in (0, 1):
                part = pl.ds(pl.multiple_of(n * 512, 512), 512)
                dkv_ref[s, part, :] = acc_ref[s, part, :].astype(BF)

    return pl.pallas_call(
        kernel,
        in_specs=[SMEM, SMEM] + [VMEM] * 5,
        out_specs=(VMEM, VMEM),
        scratch_shapes=[pltpu.VMEM((2, 8192, 128), F32), pltpu.SMEM((64,), jnp.int32)],
        out_shape=(shaped((1024, 128), F32), shaped((2, 8192, 128), BF)),
        compiler_params=pltpu.CompilerParams(vmem_limit_bytes=LIMIT),
        name="attend_back",
    )(lengths, order, q, kv, d_att, att, lse)


def hand_out(parts):
    def kernel(*refs):
        n = len(refs) // 2
        for k, (src, dst) in enumerate(zip(refs[:n], refs[n:])):
            if dst.shape == (15,):
                wide = jnp.concatenate([src[...], jnp.zeros((113, 128), F32)], axis=0)
                dst[...] = wide.T[0:1, 0:15].reshape(15)
            else:
                dst[...] = src[...]

    shapes = [(15,) if v.shape == (15, 128) else v.shape for v in parts]
    return pl.pallas_call(
        kernel,
        out_shape=tuple(shaped(s, v.dtype) for s, v in zip(shapes, parts)),
        in_specs=[VMEM] * len(parts),
        out_specs=(VMEM,) * len(parts),
        compiler_params=pltpu.CompilerParams(vmem_limit_bytes=LIMIT),
        name="hand_out",
    )(*parts)


def local(
    hidden, attn_gain, w_q, w_k, w_v, w_o, mlp_gain, w_gate, w_up, w_down, cotangent,
    doc_lengths, span_order,
):
    frequency = ROPE_BASE ** (-2.0 * (np.arange(128) % 32) / HEAD)
    frequency = jnp.asarray(frequency, F32).reshape(1, 128)

    rows, w1, wds, wo, cot, w2own, normed, q, kv, cos_t, sin_t = first(
        hidden.T, cotangent.T, w_q, w_k, w_v, w_o, w_gate, w_up, w_down, attn_gain, mlp_gain,
        doc_lengths, span_order, frequency,
    )
    kv = kv.reshape(2, 8192, 128)
    att, lse = attend(doc_lengths, span_order, q, kv)
    output, d_resid, d_heads, gwo, gw2s, gwds = feed(
        att, w2own, wo, rows.reshape(1024, WIDE), wds.reshape(384, WIDE), cot.reshape(1024, WIDE)
    )
    d_att = d_heads.reshape(1024, 128)
    dq, dkv = attend_back(doc_lengths, span_order, q, kv, d_att, att, lse)
    grads = last(
        dkv.reshape(2, 8, 1024, 128), gwo, dq, cos_t, sin_t, w1.reshape(WIDE, 256), normed, rows,
        d_resid, gw2s, gwds, attn_gain, mlp_gain, w_q, w_k, w_v, w_gate, w_up,
    )
    output, grad_hidden, g_attn, g_mlp, g_q, g_k, g_v, g_o, g_gate, g_up, g_down = hand_out(
        (output,) + tuple(grads)
    )
    return (
        output.T, grad_hidden.T, g_attn, g_q, g_k, g_v, g_o, g_mlp, g_gate, g_up, g_down
    )


def solution(mesh):
    both = ("fsdp", "ctx")
    wide, thin, part = P(both, None), P(both), P("fsdp")
    return jax.shard_map(
        local,
        mesh=mesh,
        in_specs=(wide, thin, wide, wide, wide, wide, thin, wide, wide, wide, wide, part, part),
        out_specs=(wide, wide, thin, wide, wide, wide, wide, thin, wide, wide, wide),
        check_vma=False,
    )
```

profile of v0, /device:TPU:32, one launch (start us, length us, event | category | flops | bytes accessed | tf_op | source)
XLA Modules:
  0.0 206.7 jit_solution(10478626063816801094)
XLA Ops:
  0.6 50.5 %first.1 = (bf16[8,128,1024]{2,1,0:T(8,128)(2,1)}, bf16[8,8,16,256]{3,2,1,0:T(8,128)(2,1)}, bf16[8,48,1024]{2,1,0:T(8,128)(2,1)}, bf16[8,8,16,1024]{3,2,1,0:T(8,...) custom-call(bf16[960,128]{1,0:T(8,128)(2,1)} %bitcast.19, ...), custom_call_target="tpu_custom_call" | custom-call | tf_op jit(solution)/shard_map/first/pallas_call | solution.py:370
  51.1 17.1 %attend.1 = (bf16[1024,128]{1,0:T(8,128)(2,1)}, f32[8,8,128]{2,1,0:T(8,128)}) custom-call(s32[3]{0:T(128)} %lengths.5, s32[64]{0:T(128)} %order.5, bf16[2,1024,128]{2,1,0:T(8,128)(2,1)} %get-tuple-element.53.q_ref, bf16[2,8192,128]{2,1,0:T(8,128)(2,1)} %bitcast.11), custom_call_target="tpu_custom_call" | custom-call | tf_op jit(solution)/shard_map/attend/pallas_call | solution.py:1151
  68.2 60.2 %feed.1 = (bf16[960,128]{1,0:T(8,128)(2,1)}, f32[128,1024]{1,0:T(8,128)}, bf16[8,128,128]{2,1,0:T(8,128)(2,1)}, bf16[8,128,1024]{2,1,0:T(8,128)(2,1)}, bf16[8,16,768]{2,1,0:T(8,128)(2,1)}, /*index=5*/f32[48,1024]{1,0:T(8,128)}) custom-call(bf16[1024,128]{1,0:T(8,128)(2,1)} %get-tuple-element.55.att.o_ref, bf16[8,16,768]{2,1,0:T(8,128)(2,1)} %get-tuple-element.56.w2own, ...), custom_call_target="tpu_custom_call" | custom-call | tf_op jit(solution)/shard_map/feed/pallas_call | solution.py:370
  128.4 21.7 %attend_back.1 = (f32[1024,128]{1,0:T(8,128)}, bf16[2,8192,128]{2,1,0:T(8,128)(2,1)}) custom-call(s32[3]{0:T(128)} %lengths.5, s32[64]{0:T(128)} %order.5, bf16[2,1024,128]{2,1,0:T(8,128)(2,1)} %get-tuple-element.53.q_ref, bf16[2,8192,128]{2,1,0:T(8,128)(2,1)} %bitcast.12, bf16[1024,128]{1,0:T(8,128)(2,1)} %bitcast.18, ...), custom_call_target="tpu_custom_call" | custom-call | tf_op jit(solution)/shard_map/attend_back/pallas_call | solution.py:1225
  150.1 53.9 %last.1 = (bf16[960,128]{1,0:T(8,128)(2,1)}, f32[15,128]{1,0:T(8,128)}, f32[15,128]{1,0:T(8,128)}, f32[15,960]{1,0:T(8,128)}, f32[15,320]{1,0:T(8,128)}, /*index...) custom-call(bf16[2,8,1024,128]{3,2,1,0:T(8,128)(2,1)} %bitcast.14, ...), custom_call_target="tpu_custom_call" | custom-call | tf_op jit(solution)/shard_map/last/pallas_call | solution.py:370
  204.1 2.4 %hand_out.1 = (bf16[960,128]{1,0:T(8,128)(2,1)}, bf16[960,128]{1,0:T(8,128)(2,1)}, f32[15]{0:T(128)}, f32[15]{0:T(128)}, f32[15,960]{1,0:T(8,128)}, /*index=5*/f...) custom-call(bf16[960,128]{1,0:T(8,128)(2,1)} %get-tuple-element.61.r, ...), custom_call_target="tpu_custom_call" | custom-call | tf_op jit(solution)/shard_map/hand_out/pallas_call | solution.py:1247
where the time goes:
time: 209 us; the launch traced here: 207 us
  Pallas kernels  206 us (99%)
    pallas_call x3, Pallas kernels, comm_call(): pl.pallas_call(kernel, out_shape=out_shape, in_specs=in_specs, out_specs=...  165 us
    pallas_call x1, Pallas kernels, attend_back(): pl.pallas_call(kernel, in_specs=[SMEM, SMEM] + [VMEM] * 5, out_specs=(VME...  21.7 us
    pallas_call x1, Pallas kernels, attend(): pl.pallas_call(kernel, in_specs=[SMEM, SMEM, VMEM, VMEM], out_specs=(VMEM...  17.1 us

commit v1 on v0

--- a/solution.py
+++ b/solution.py
@@ -143,15 +143,57 @@
         self.sent()
 
 
-def run_ring_gathers(rings):
-    for ring in rings:
-        ring.relay_z()
-    for k in (0, 1):
-        for ring in rings:
-            ring.relay_x(k)
-    for k in (0, 1):
-        for ring in rings:
-            ring.land(k)
+class CrossGather:
+    sems = [DMA((8,)), DMA((8,)), DMA(())]
+
+    def __init__(self, src, dst, half, ssem, rsem, lsem, arrived=None):
+        self.src, self.dst, self.half = src, dst, half
+        self.ssem, self.rsem, self.lsem = ssem, rsem, lsem
+        self.arrived = arrived or (lambda block: None)
+        self.copies = {}
+
+    def push(self, n, src, dst, device):
+        self.copies[n] = send(src, dst, self.ssem.at[n], self.rsem.at[n], device)
+
+    def start(self):
+        x, z, y, c = place()
+        me = self.dst.at[x * 2 + z]
+        self.push(1, self.src, me, at(x + 1, z, y, c))
+        self.push(2, self.src, me, at(x - 1, z, y, c))
+        self.push(0, self.src, me, at(x, 1 - z, y, c))
+        self.local = pltpu.make_async_copy(self.src, me, self.lsem)
+        self.local.start()
+
+    def relay(self):
+        x, z, y, c = place()
+        for n, step, side in ((1, 3, 0), (2, 1, 1)):
+            block = ((x + step) % 4) * 2 + z
+            whole = self.dst.at[block]
+            self.copies[n].wait_recv()
+            part = self.half(whole, side)
+            self.push(2 + n, part, part, at(x + 4 - step, z, y, c))
+            self.push(4 + n, whole, whole, at(x, 1 - z, y, c))
+            self.arrived(block)
+
+    def far(self):
+        x, z, y, c = place()
+        block = ((x + 2) % 4) * 2 + z
+        whole = self.dst.at[block]
+        self.copies[3].wait_recv()
+        self.copies[4].wait_recv()
+        self.push(7, whole, whole, at(x, 1 - z, y, c))
+        self.arrived(block)
+
+    def land(self):
+        x, z, y, c = place()
+        for n, step in ((0, 0), (5, 3), (6, 1), (7, 2)):
+            self.copies[n].wait_recv()
+            self.arrived(((x + step) % 4) * 2 + 1 - z)
+
+    def finish(self):
+        self.local.wait()
+        for n in range(8):
+            self.copies[n].wait_send()
 
 
 class RowGather:
@@ -238,13 +280,15 @@
         return [
             pltpu.VMEM((4,) + shape, BF),
             pltpu.VMEM((4,) + shape, BF),
-            pltpu.VMEM((4,) + shape, BF),
+            pltpu.VMEM((2, shape[0] // 2) + shape[1:], BF),
+            pltpu.VMEM((2,) + shape, BF),
             DMA((8,)),
             DMA((8,)),
         ]
 
-    def __init__(self, blk, first, mixed, second, ssem, rsem):
-        self.blk, self.first, self.mixed, self.second = blk, first, mixed, second
+    def __init__(self, blk, first, mixed, parts, heard, ssem, rsem):
+        self.blk, self.first, self.mixed = blk, first, mixed
+        self.parts, self.heard = parts, heard
         self.ssem, self.rsem = ssem, rsem
         self.copies = {}
 
@@ -260,25 +304,102 @@
         for d in (2, 1, 3, 0):
             self.hand(d)
 
-    def relay(self):
-        x, z, y, c = place()
-        for d in (2, 1, 3):
-            self.copies[d].wait_recv()
-            own = self.blk[((y + d) % 4) * 2 + c].astype(F32)
-            self.mixed[d] = (own + self.first[d].astype(F32)).astype(BF)
-            self.push(4 + d, self.mixed.at[d], self.second.at[d], at(x, z, y + d, c))
+    def both(self, d):
+        x, z, y, c = place()
+        self.copies[d].wait_recv()
+        return self.blk[((y + d) % 4) * 2 + c].astype(F32) + self.first[d].astype(F32)
+
+    def far(self):
+        x, z, y, c = place()
+        self.mixed[2] = self.both(2).astype(BF)
+        for side, step in ((0, 1), (1, 3)):
+            part = half_lead(self.mixed.at[2], side)
+            self.push(4 + side, part, self.parts.at[side], at(x, z, y + step, c))
+
+    def near(self):
+        x, z, y, c = place()
+        for side, step in ((0, 1), (1, 3)):
+            sums = self.both(step)
+            n = sums.shape[0] // 2
+            self.copies[4 + side].wait_recv()
+            part = self.parts[side].astype(F32)
+            self.mixed[step, pl.ds(side * n, n)] = (sums[side * n : side * n + n] + part).astype(BF)
+            self.mixed[step, pl.ds(n - side * n, n)] = sums[n - side * n : 2 * n - side * n].astype(BF)
+            self.push(6 + side, self.mixed.at[step], self.heard.at[side], at(x, z, y + step, c))
 
     def total(self):
-        x, z, y, c = place()
-        self.copies[0].wait_recv()
-        total = self.blk[y * 2 + c].astype(F32) + self.first[0].astype(F32)
-        for d in (1, 3, 2):
-            self.copies[4 + d].wait_recv()
-            total = total + self.second[d].astype(F32)
+        total = self.both(0)
+        for side in (0, 1):
+            self.copies[6 + side].wait_recv()
+            total = total + self.heard[side].astype(F32)
         return total
 
     def finish(self):
-        for n in (0, 1, 2, 3, 5, 6, 7):
+        for n in range(8):
+            self.copies[n].wait_send()
+
+
+class CrossSum:
+    @staticmethod
+    def scratch(shape, lanes):
+        if lanes:
+            part = shape[:-1] + (shape[-1] // 2,)
+        else:
+            part = (shape[0] // 2,) + shape[1:]
+        return [
+            pltpu.VMEM((4,) + shape, BF),
+            pltpu.VMEM((4,) + shape, BF),
+            pltpu.VMEM((2,) + part, BF),
+            pltpu.VMEM((2,) + shape, BF),
+            DMA((8,)),
+            DMA((8,)),
+        ]
+
+    def __init__(self, blk, lanes, first, mixed, parts, heard, ssem, rsem):
+        self.blk, self.half = blk, half_lanes if lanes else half_lead
+        self.first, self.mixed, self.parts, self.heard = first, mixed, parts, heard
+        self.ssem, self.rsem = ssem, rsem
+        self.copies = {}
+
+    def push(self, n, src, dst, device):
+        self.copies[n] = send(src, dst, self.ssem.at[n], self.rsem.at[n], device)
+
+    def hand(self, d):
+        x, z, y, c = place()
+        to = ((x + d) % 4) * 2 + 1 - z
+        self.push(d, self.blk.at[to], self.first.at[d], at(x, 1 - z, y, c))
+
+    def both(self, d):
+        x, z, y, c = place()
+        self.copies[d].wait_recv()
+        return self.blk[((x + d) % 4) * 2 + z].astype(F32) + self.first[d].astype(F32)
+
+    def far(self):
+        x, z, y, c = place()
+        self.mixed[2] = self.both(2).astype(BF)
+        for side, step in ((0, 1), (1, 3)):
+            part = self.half(self.mixed.at[2], side)
+            self.push(4 + side, part, self.parts.at[side], at(x + step, z, y, c))
+
+    def near(self):
+        x, z, y, c = place()
+        for side, step in ((0, 1), (1, 3)):
+            mixed = self.mixed.at[step]
+            mixed[...] = self.both(step).astype(BF)
+            self.copies[4 + side].wait_recv()
+            mine = self.half(mixed, side)
+            mine[...] = (mine[...].astype(F32) + self.parts[side].astype(F32)).astype(BF)
+            self.push(6 + side, mixed, self.heard.at[side], at(x + step, z, y, c))
+
+    def total(self):
+        total = self.both(0)
+        for side in (0, 1):
+            self.copies[6 + side].wait_recv()
+            total = total + self.heard[side].astype(F32)
+        return total
+
+    def finish(self):
+        for n in range(8):
             self.copies[n].wait_send()
 
 
@@ -421,29 +542,33 @@
         spread = spread_value(WIDTH)
         xp[...] = dot_tn(hidden_t[...], spread).astype(BF)
 
+        wop[...] = jnp.zeros(wop.shape, BF)
+        wop[0:15, :] = dot(w_o[...], spread).astype(BF)
+        wdp[...] = jnp.zeros(wdp.shape, BF)
+        wdp[0:40, :] = dot(w_down[...], spread).astype(BF)
+
         pl.semaphore_wait(pltpu.get_barrier_semaphore(), partners)
         swap = Swap(wp1, w1own, *b)
         swap.start()
         gather = RowGather(xp, rows, *a)
         gather.start()
-        wop[...] = jnp.zeros(wop.shape, BF)
-        wop[0:15, :] = dot(w_o[...], spread).astype(BF)
-        wdp[...] = jnp.zeros(wdp.shape, BF)
-        wdp[0:40, :] = dot(w_down[...], spread).astype(BF)
-        ring_o = RingGather(wop, wos, half_lanes, *e)
-        ring_d = RingGather(wdp, wds, half_lanes, *e2)
+        early = [RingGather(wdp, wds, half_lanes, *e2), RingGather(wop, wos, half_lanes, *e)]
+        ring_d, ring_o = early
+        for ring in early:
+            ring.start()
+        cp[...] = dot_tn(cot_t[...], spread).astype(BF)
+        for ring in early:
+            ring.relay_z()
         swap.finish()
         ring_1 = RingGather(w1own, w1, half_lead, *d)
         ring_1.start()
-        ring_o.start()
-        ring_d.start()
-        cp[...] = dot_tn(cot_t[...], spread).astype(BF)
+        for k in (0, 1):
+            for ring in early:
+                ring.relay_x(k)
         gather.relay()
         gather_c = RowGather(cp, cot, *ac)
         gather_c.start()
-        rings = [ring_1, ring_o, ring_d]
-        for ring in rings:
-            ring.relay_z()
+        ring_1.relay_z()
 
         wp2[...] = jnp.zeros(wp2.shape, BF)
         gap = jnp.zeros((15, 8), F32)
@@ -455,12 +580,8 @@
                     n = (8 * g + f) * 40
                     parts += [w[:, n : n + 40], gap]
                 wp2[f, 0:15, m : m + 384] = jnp.concatenate(parts, axis=1).astype(BF)
-        swap2 = Swap(wp2, w2own, *b2)
-        swap2.start()
-
-        for k in (0, 1):
-            for ring in rings:
-                ring.relay_x(k)
+        ring_1.relay_x(0)
+        ring_1.relay_x(1)
 
         lane = lanes_of((1, 128))
         sign = jnp.where(lane % 64 < 32, -1.0, 1.0)
@@ -478,12 +599,14 @@
         written = [fetch(cos_t, cos_out, outs.at[0]), fetch(sin_t, sin_out, outs.at[1])]
         gather.land()
         for k in (0, 1):
-            for ring in rings:
+            for ring in early + [ring_1]:
                 ring.land(k)
+        gather.finish()
         ring_o.local.wait()
         gather_o = RowGather(wos, wo, *ao)
         gather_o.start()
-        gather.finish()
+        swap2 = Swap(wp2, w2own, *b2)
+        swap2.start()
         ring_1.local.wait()
         written += [fetch(rows, rows_out, outs.at[2]), fetch(w1, w1_out, outs.at[3])]
 
@@ -510,10 +633,10 @@
             hand.append(send(piece, piece, hs.at[n], hr.at[n], at(x, z, y, 1 - c)))
 
         key_rings = []
-        for h, own in ((0, k0), (1, k1)):
+        for h, (kind, own) in enumerate(((RingGather, k0), (CrossGather, k1))):
             mine = kv.at[pl.ds(512 * h, 512)]
             spot = pl.ds(512 * h, 512)
-            ring = RingGather(
+            ring = kind(
                 mine,
                 kv2.at[c, :, spot],
                 half_lead,
@@ -534,18 +657,18 @@
                 gather_c.relay()
 
         written += [fetch(normed, normed_out, outs.at[4]), fetch(q_rot, q_out, outs.at[5])]
-        for ring in key_rings:
-            ring.relay_z()
+        ring_a, ring_b = key_rings
+        ring_a.relay_z()
         gather_o.relay()
-        for ring in key_rings:
-            ring.relay_x(0)
+        ring_b.relay()
+        ring_a.relay_x(0)
         gather_c.land()
-        for ring in key_rings:
-            ring.relay_x(1)
+        ring_a.relay_x(1)
+        ring_b.far()
         gather_o.land()
-        for k in (0, 1):
-            for ring in key_rings:
-                ring.land(k)
+        ring_a.land(0)
+        ring_a.land(1)
+        ring_b.land()
         for copy in hand:
             copy.wait()
         swap2.finish()
@@ -600,7 +723,8 @@
         + RingGather.sems * 3
         + RowGather.sems * 2
         + Swap.sems
-        + RingGather.sems * 2
+        + RingGather.sems
+        + CrossGather.sems
         + [DMA((16,)), DMA((16,))],
         (
             hidden_t, cot_t, w_q, w_k, w_v, w_o, w_gate, w_up, w_down, gain1, gain2, lengths,
@@ -616,11 +740,11 @@
 def feed(att, w2own, wo, rows, wd, cot):
     def kernel(
         att, w2own, wo_in, rows_in, wd_in, cot_in,
-        output, d_resid, d_heads, gwo_out, gw2_sum, gwd_sum,
+        outp_out, resid_out, d_resid, d_heads, gwo_out, gw2_sum, gwd_sum,
         wo, x_in, wd, cot, ins, atts, w2, packed, d_act, resid, normed, act, d_both, dmn, outp,
         gw2, gwd, da, gwo, *refs,
     ):
-        a, b, s, r1, r2, t1, t2 = split(refs, (3, 3, 3, 5, 5, 6, 6))
+        a, b, s, r1, t1, t2 = split(refs, (3, 3, 3, 6, 6, 6))
         x, z, y, c = place()
         me = y * 2 + c
         partners = hail("xf")
@@ -689,8 +813,8 @@
             d_both[part, 0:384] = (d * up * sigma * (1.0 + gate * (1.0 - sigma))).astype(BF)
             d_both[part, 384:768] = (d * silu).astype(BF)
 
-        sum_n, sum_o = RowSum(dmn, *r1), RowSum(outp, *r2)
-        ring_2, ring_d = RingSum(gw2, False, *t1), RingSum(gwd, True, *t2)
+        sum_n = RowSum(dmn, *r1)
+        ring_2, ring_d = RingSum(gw2, False, *t1), CrossSum(gwd, True, *t2)
 
         def back(core):
             to = [((y + n) % 4) * 2 + core for n in (2, 1, 3, 0)]
@@ -715,13 +839,14 @@
         for d in (2, 1, 3, 0):
             sum_n.hand(d)
         gwd[...] = dot_tn(act[...], cot[...]).astype(BF).reshape(8, 48, WIDE)
-        ring_d.start(0)
-        ring_d.start(1)
+        for d in (2, 1, 3, 0):
+            ring_d.hand(d)
         back(c)
-        sum_n.relay()
+        sum_n.far()
         weights((2, 3, 4, 5, 6, 7))
+        sum_n.near()
         ring_2.relay(0)
-        ring_d.relay(0)
+        ring_d.far()
 
         @pl.loop(0, 2)
         def _(n):
@@ -729,10 +854,9 @@
             for k in range(4):
                 outp[n * 4 + k] = v[128 * k : 128 * k + 128]
 
-        sum_o.start()
+        written = [fetch(outp, outp_out, ins.at[5])]
         ring_2.relay(1)
-        ring_d.relay(1)
-        sum_o.relay()
+        ring_d.near()
 
         mine = place_rows(me, 128)
         v = resid[mine, :]
@@ -754,25 +878,25 @@
             for f in range(8):
                 n = (8 * g + f) * 16
                 gwo[f, g * 16 : (g + 1) * 16, :] = gw[n : n + 16]
-        written = fetch(gwo, gwo_out, ins.at[4])
+        written += [fetch(gwo, gwo_out, ins.at[4])]
         ring_2.total(0)
-        ring_d.total(0)
-        output[...] = dot_nt(spread[0:WIDTH], (v + sum_o.total()).astype(BF)).astype(BF)
+        resid_out[...] = v
         gw2_sum[...] = ring_2.total(1).astype(BF)
-        gwd_sum[...] = ring_d.total(1)
+        gwd_sum[...] = ring_d.total()
         swap.finish()
         sum_n.finish()
-        sum_o.finish()
         ring_2.finish()
         ring_d.finish()
-        written.wait()
+        for copy in written:
+            copy.wait()
 
     return comm_call(
         "feed",
         3,
         kernel,
         (
-            shaped((WIDTH, 128), BF),
+            shaped((8, 128, WIDE), BF),
+            shaped((128, WIDE), F32),
             shaped((128, WIDE), F32),
             shaped((8, 128, 128), BF),
             shaped((8, 128, WIDE), BF),
@@ -780,13 +904,13 @@
             shaped((48, WIDE), F32),
         ),
         [ANY] * 6,
-        (VMEM, VMEM, ANY, ANY, VMEM, VMEM),
+        (ANY, VMEM, VMEM, ANY, ANY, VMEM, VMEM),
         [
             pltpu.VMEM((8, 8, 16, WIDE), BF),
             pltpu.VMEM((1024, WIDE), BF),
             pltpu.VMEM((384, WIDE), BF),
             pltpu.VMEM((1024, WIDE), BF),
-            DMA((5,)),
+            DMA((6,)),
             pltpu.VMEM((8, 1024, 128), BF),
             pltpu.VMEM((8, 8, 16, 768), BF),
             pltpu.VMEM((WIDE, WIDE), BF),
@@ -805,25 +929,26 @@
         + RowGather.sems
         + RingGather.sems
         + Swap.sems
-        + RowSum.scratch((128, WIDE)) * 2
+        + RowSum.scratch((128, WIDE))
         + RingSum.scratch((8, 16, 768), False)
-        + RingSum.scratch((48, WIDE), True),
+        + CrossSum.scratch((48, WIDE), True),
         (att, w2own, wo, rows, wd, cot),
     )
 
 
 def last(
-    dkv, gwo, dq, cos_t, sin_t, w1, normed, rows, d_resid, gw2s, gwd, gain1, gain2, w_q, w_k, w_v,
-    w_gate, w_up,
+    dkv, gwo, outp, dq, cos_t, sin_t, w1, normed, rows, resid, d_resid, gw2s, gwd, gain1, gain2,
+    w_q, w_k, w_v, w_gate, w_up,
 ):
     def kernel(
-        dkv, gwo_in, dq_in, cos_in, sin_in, w1_in, normed_in, rows_in, dr, gw2s, wd, gain1, gain2,
+        dkv, gwo_in, outp_in, dq_in, cos_in, sin_in, w1_in, normed_in, rows_in, resid, dr, gw2s, wd,
+        gain1, gain2,
         w_q, w_k, w_v, w_gate, w_up,
-        gh, g_attn, g_mlp, g_q, g_k, g_v, g_o, g_gate, g_up, g_down,
-        own, gwo, dq, cos_t, sin_t, w1, normed, rows, ins,
-        blk, from_core, gwos, gw1, dnq, d_kv, dn, one, two, gw1s, hs, hr, *refs,
+        output, gh, g_attn, g_mlp, g_q, g_k, g_v, g_o, g_gate, g_up, g_down,
+        own, gwo, outp, dq, cos_t, sin_t, w1, normed, rows, ins,
+        blk_a, blk_b, from_core, gwos, gw1, dnq, d_kv, dn, one, two, gw1s, hs, hr, *refs,
     ):
-        a, b, d, e, e2, s1, s2 = split(refs, (6, 5, 5, 6, 6, 3, 3))
+        a, a2, b, b2, d, e, e2, s1, s2 = split(refs, (6, 6, 6, 6, 6, 6, 6, 3, 3))
         x, z, y, c = place()
         me = y * 2 + c
         partners = hail("xf")
@@ -836,35 +961,44 @@
             (w1_in, w1),
             (normed_in, normed),
             (rows_in.at[me], rows),
+            (outp_in, outp),
         ]
         held = [fetch(src, dst, ins.at[n]) for n, (src, dst) in enumerate(pairs)]
         pl.semaphore_wait(pltpu.get_barrier_semaphore(), partners)
-        order = [(2, 1), (2, 0), (1, 1), (3, 1), (1, 0), (3, 0), (0, 1), (0, 0)]
+        order = [(2, 1), (2, 0), (1, 1), (3, 1), (0, 1), (1, 0), (3, 0), (0, 0)]
         where = [((x + p) % 4) * 2 + (1 - z if q else z) for p, q in order]
         hand = [
             send(dkv.at[1 - c, g], from_core.at[n], hs.at[n], hr.at[n], at(x, z, y, 1 - c))
             for n, g in enumerate(where)
         ]
+        ring_a, ring_b = RingSum(blk_a, False, *a), CrossSum(blk_b, False, *a2)
+        held[1].wait()
+
+        def fold(n):
+            g = where[n]
+            hand[n].wait_recv()
+            both = (own[g].astype(F32) + from_core[n].astype(F32)).astype(BF)
+            blk_a[g] = both[0:512]
+            blk_b[g] = both[512:1024]
+
+        fold(0)
+        ring_a.start(0)
+        ring_b.hand(2)
+        fold(1)
+        ring_a.start(1)
+        for n, step in ((2, 1), (3, 3), (4, 0)):
+            fold(n)
+            ring_b.hand(step)
+        for n in (5, 6, 7):
+            fold(n)
         held[0].wait()
         sum_w = RowSum(gwo, *b)
         sum_w.start()
         swap2 = Swap(gw2s, two, *s2)
         swap2.start()
-        ring = RingSum(blk, False, *a)
-        held[1].wait()
-
-        def fold(n):
-            g = where[n]
-            hand[n].wait_recv()
-            blk[g] = (own[g].astype(F32) + from_core[n].astype(F32)).astype(BF)
-
-        fold(0)
-        ring.start(0)
-        fold(1)
-        ring.start(1)
-        for n in range(2, 6):
-            fold(n)
-        sum_w.relay()
+        held[8].wait()
+        sum_o = RowSum(outp, *b2)
+        sum_o.start()
         for n in range(2, 6):
             held[n].wait()
         spread = spread_value(WIDTH)
@@ -881,20 +1015,21 @@
             dnq[part, :] = dot_nt(v, w1[:, 0:128])
 
         queries(0)
-        ring.relay(0)
+        ring_a.relay(0)
+        sum_w.far()
+        ring_b.far()
         queries(1)
-        ring.relay(1)
-        fold(6)
-        fold(7)
+        ring_a.relay(1)
+        sum_o.far()
+        sum_w.near()
+        ring_b.near()
         held[6].wait()
         gw1[:, :, :, 0:128] = (
             dot_tn(normed[...], d_kv[:, 0:128]).astype(BF).reshape(8, 8, 16, 128)
         )
+        ring_a.total(0)
+        sum_o.near()
         gwos[...] = sum_w.total().astype(BF).reshape(8, 16, WIDE)
-        ring_o = RingSum(gwos, True, *e2)
-        ring_o.start(0)
-        ring_o.start(1)
-        ring.total(0)
         swap2.finish()
         total = jnp.zeros((15, 1), F32)
         for m, ref, w in ((0, g_gate, w_gate), (384, g_up, w_up)):
@@ -918,10 +1053,9 @@
             return dot_nt(top, spread) + dot_nt(low, spread)
 
         g_down[...] = squeeze(wd[...])[0:40]
-        ring_o.relay(0)
-        ring_o.relay(1)
-
-        v = ring.total(1)
+        output[...] = dot_nt(spread, (resid[...] + sum_o.total()).astype(BF)).astype(BF)
+
+        v = jnp.concatenate([ring_a.total(1), ring_b.total()], axis=0)
         turned = v * cos_t[...] - partner(v) * sin_t[...]
         d_kv[:, 128:256] = jnp.where(lanes_of((1024, 128)) < 64, turned, v).astype(BF)
         sum_n = RowSum(dn, *d)
@@ -949,17 +1083,22 @@
         weights_k((0, 1))
         ring_1.start(0)
         ring_1.start(1)
+        ring_o = RingSum(gwos, True, *e2)
+        ring_o.start(0)
+        ring_o.start(1)
         back(c)
-        sum_n.relay()
+        sum_n.far()
         weights_k((2, 3, 4, 5, 6, 7))
-        ring_1.relay(0)
-        ring_1.relay(1)
+        sum_n.near()
+        for k in (0, 1):
+            ring_1.relay(k)
+            ring_o.relay(k)
+        ring_1.total(0)
         ring_o.total(0)
-        ring_1.total(0)
-        g_o[...] = squeeze(ring_o.total(1))[0:15]
         gw1s[...] = ring_1.total(1).astype(BF)
         swap1 = Swap(gw1s, one, *s1)
         swap1.start()
+        g_o[...] = squeeze(ring_o.total(1))[0:15]
 
         held[7].wait()
         xs = rows[...].astype(F32)
@@ -988,10 +1127,12 @@
         g_attn[...] = jnp.broadcast_to(total, (15, 128))
         for copy in hand:
             copy.wait_send()
-        ring.finish()
+        ring_a.finish()
+        ring_b.finish()
         ring_1.finish()
         ring_o.finish()
         sum_w.finish()
+        sum_o.finish()
         sum_n.finish()
 
     return comm_call(
@@ -999,6 +1140,7 @@
         6,
         kernel,
         (
+            shaped((WIDTH, 128), BF),
             shaped((WIDTH, 128), BF),
             shaped((15, 128), F32),
             shaped((15, 128), F32),
@@ -1010,10 +1152,11 @@
             shaped((15, 2560), F32),
             shaped((40, WIDTH), F32),
         ),
-        [ANY] * 8 + [VMEM] * 10,
-        (VMEM,) * 10,
+        [ANY] * 9 + [VMEM] * 11,
+        (VMEM,) * 11,
         [
             pltpu.VMEM((8, 1024, 128), BF),
+            pltpu.VMEM((8, 128, WIDE), BF),
             pltpu.VMEM((8, 128, WIDE), BF),
             pltpu.VMEM((1024, 128), F32),
             pltpu.VMEM((1024, 128), F32),
@@ -1021,8 +1164,9 @@
             pltpu.VMEM((WIDE, 256), BF),
             pltpu.VMEM((1024, WIDE), BF),
             pltpu.VMEM((128, WIDE), BF),
-            DMA((8,)),
-            pltpu.VMEM((8, 1024, 128), BF),
+            DMA((9,)),
+            pltpu.VMEM((8, 512, 128), BF),
+            pltpu.VMEM((8, 512, 128), BF),
             pltpu.VMEM((8, 1024, 128), BF),
             pltpu.VMEM((8, 16, WIDE), BF),
             pltpu.VMEM((8, 8, 16, 256), BF),
@@ -1035,14 +1179,15 @@
             DMA((8,)),
             DMA((8,)),
         ]
-        + RingSum.scratch((1024, 128), False)
-        + RowSum.scratch((128, WIDE)) * 2
+        + RingSum.scratch((512, 128), False)
+        + CrossSum.scratch((512, 128), False)
+        + RowSum.scratch((128, WIDE)) * 3
         + RingSum.scratch((8, 16, 256), False)
         + RingSum.scratch((16, WIDE), True)
         + Swap.sems * 2,
         (
-            dkv, gwo, dq, cos_t, sin_t, w1, normed, rows, d_resid, gw2s, gwd, gain1, gain2, w_q,
-            w_k, w_v, w_gate, w_up,
+            dkv, gwo, outp, dq, cos_t, sin_t, w1, normed, rows, resid, d_resid, gw2s, gwd, gain1,
+            gain2, w_q, w_k, w_v, w_gate, w_up,
         ),
     )
 
@@ -1267,18 +1412,16 @@
     )
     kv = kv.reshape(2, 8192, 128)
     att, lse = attend(doc_lengths, span_order, q, kv)
-    output, d_resid, d_heads, gwo, gw2s, gwds = feed(
+    outp, resid, d_resid, d_heads, gwo, gw2s, gwds = feed(
         att, w2own, wo, rows.reshape(1024, WIDE), wds.reshape(384, WIDE), cot.reshape(1024, WIDE)
     )
     d_att = d_heads.reshape(1024, 128)
     dq, dkv = attend_back(doc_lengths, span_order, q, kv, d_att, att, lse)
     grads = last(
-        dkv.reshape(2, 8, 1024, 128), gwo, dq, cos_t, sin_t, w1.reshape(WIDE, 256), normed, rows,
-        d_resid, gw2s, gwds, attn_gain, mlp_gain, w_q, w_k, w_v, w_gate, w_up,
+        dkv.reshape(2, 8, 1024, 128), gwo, outp, dq, cos_t, sin_t, w1.reshape(WIDE, 256), normed,
+        rows, resid, d_resid, gw2s, gwds, attn_gain, mlp_gain, w_q, w_k, w_v, w_gate, w_up,
     )
-    output, grad_hidden, g_attn, g_mlp, g_q, g_k, g_v, g_o, g_gate, g_up, g_down = hand_out(
-        (output,) + tuple(grads)
-    )
+    output, grad_hidden, g_attn, g_mlp, g_q, g_k, g_v, g_o, g_gate, g_up, g_down = hand_out(grads)
     return (
         output.T, grad_hidden.T, g_attn, g_q, g_k, g_v, g_o, g_mlp, g_gate, g_up, g_down
     )

time: 209 us -> 205 us (0.981)
    pallas_call x3, Pallas kernels: 165 us -> 155 us  [comm_call(): pl.pallas_call(kernel, out_shape=out_shape, in_specs=in_specs, out_specs=...]
    pallas_call x1, Pallas kernels: 21.7 us -> 25.9 us  [attend_back(): pl.pallas_call(kernel, in_specs=[SMEM, SMEM] + [VMEM] * 5, out_specs=(VME...]
    pallas_call x1, Pallas kernels: 17.1 us -> 20.5 us  [attend(): pl.pallas_call(kernel, in_specs=[SMEM, SMEM, VMEM, VMEM], out_specs=(VMEM...]
where the time goes in v1:
time: 205 us; the launch traced here: 204 us
  Pallas kernels  204 us (100%)
    pallas_call x3, Pallas kernels, comm_call(): pl.pallas_call(kernel, out_shape=out_shape, in_specs=in_specs, out_specs=...  155 us
    pallas_call x1, Pallas kernels, attend_back(): pl.pallas_call(kernel, in_specs=[SMEM, SMEM] + [VMEM] * 5, out_specs=(VME...  25.9 us
    pallas_call x1, Pallas kernels, attend(): pl.pallas_call(kernel, in_specs=[SMEM, SMEM, VMEM, VMEM], out_specs=(VMEM...  20.5 us

profile of v1, /device:TPU:32, one launch (start us, length us, event | category | flops | bytes accessed | tf_op | source)
XLA Modules:
  0.0 204.4 jit_solution(718373146571109246)
XLA Ops:
  0.6 48.6 %first.1 = (bf16[8,128,1024]{2,1,0:T(8,128)(2,1)}, bf16[8,8,16,256]{3,2,1,0:T(8,128)(2,1)}, bf16[8,48,1024]{2,1,0:T(8,128)(2,1)}, bf16[8,8,16,1024]{3,2,1,0:T(8,...) custom-call(bf16[960,128]{1,0:T(8,128)(2,1)} %bitcast.19, ...), custom_call_target="tpu_custom_call" | custom-call | tf_op jit(solution)/shard_map/first/pallas_call | solution.py:491
  49.3 20.5 %attend.1 = (bf16[1024,128]{1,0:T(8,128)(2,1)}, f32[8,8,128]{2,1,0:T(8,128)}) custom-call(s32[3]{0:T(128)} %lengths.5, s32[64]{0:T(128)} %order.5, bf16[2,1024,128]{2,1,0:T(8,128)(2,1)} %get-tuple-element.55.q_ref, bf16[2,8192,128]{2,1,0:T(8,128)(2,1)} %bitcast.11), custom_call_target="tpu_custom_call" | custom-call | tf_op jit(solution)/shard_map/attend/pallas_call | solution.py:1296
  69.7 52.1 %feed.1 = (bf16[8,128,1024]{2,1,0:T(8,128)(2,1)}, f32[128,1024]{1,0:T(8,128)}, f32[128,1024]{1,0:T(8,128)}, bf16[8,128,128]{2,1,0:T(8,128)(2,1)}, bf16[8,128,102...) custom-call(bf16[1024,128]{1,0:T(8,128)(2,1)} %get-tuple-element.57.att.o_ref, ...), custom_call_target="tpu_custom_call" | custom-call | tf_op jit(solution)/shard_map/feed/pallas_call | solution.py:491
  121.8 25.9 %attend_back.1 = (f32[1024,128]{1,0:T(8,128)}, bf16[2,8192,128]{2,1,0:T(8,128)(2,1)}) custom-call(s32[3]{0:T(128)} %lengths.5, s32[64]{0:T(128)} %order.5, bf16[2,1024,128]{2,1,0:T(8,128)(2,1)} %get-tuple-element.55.q_ref, bf16[2,8192,128]{2,1,0:T(8,128)(2,1)} %bitcast.12, bf16[1024,128]{1,0:T(8,128)(2,1)} %bitcast.18, ...), custom_call_target="tpu_custom_call" | custom-call | tf_op jit(solution)/shard_map/attend_back/pallas_call | solution.py:1370
  147.7 54.0 %last.1 = (bf16[960,128]{1,0:T(8,128)(2,1)}, bf16[960,128]{1,0:T(8,128)(2,1)}, f32[15,128]{1,0:T(8,128)}, f32[15,128]{1,0:T(8,128)}, f32[15,960]{1,0:T(8,128)}, ...) custom-call(bf16[2,8,1024,128]{3,2,1,0:T(8,128)(2,1)} %bitcast.14, ...), custom_call_target="tpu_custom_call" | custom-call | tf_op jit(solution)/shard_map/last/pallas_call | solution.py:491
  201.7 2.4 %hand_out.1 = (bf16[960,128]{1,0:T(8,128)(2,1)}, bf16[960,128]{1,0:T(8,128)(2,1)}, f32[15]{0:T(128)}, f32[15]{0:T(128)}, f32[15,960]{1,0:T(8,128)}, /*index=5*/f...) custom-call(bf16[960,128]{1,0:T(8,128)(2,1)} %get-tuple-element.77.r, ...), custom_call_target="tpu_custom_call" | custom-call | tf_op jit(solution)/shard_map/hand_out/pallas_call | solution.py:1392
